TPU v7x, 32 devices: a whole 2x2x4 slice. The times are simulated.
32 devices in a mesh: group: 2 (over y), freq: 4 (over z), recv: 2 (over x), sub: 2 (over core).
Axes of the slice: x: 2, y: 2, z: 4, core: 2. Of those that a mesh axis runs over, the one named last changes fastest.
Arguments:
- focusing: float32 [8, 512, 8192], P(('group', 'sub'), 'freq', 'recv'), parts along dimension 0, may hold values from -6 to 6
- observed: float32 [8, 512, 8192], P(('group', 'sub'), 'freq', 'recv'), parts along dimension 0, may hold values from -6 to 6
- recv_factor: bfloat16 [4, 4, 16, 32, 8192], P('group', 'freq', 'sub', None, 'recv'), parts along dimension 0, may hold values from -0.0625 to 0.0625
- source_factor: bfloat16 [4, 4, 16, 32, 8192], P('group', 'freq', 'sub', 'recv'), parts along dimension 0, may hold values from -1.5 to 1.5
- tile_ranks: int32 [8, 32, 32], P(('group', 'freq'), 'recv'), parts along dimension 0, may hold values from 1 to 16
- window_start: int32 [8, 8192], P(('group', 'sub'), 'recv'), parts along dimension 0, may hold values from 0 to 255
- window_end: int32 [8, 8192], P(('group', 'sub'), 'recv'), parts along dimension 0, may hold values from 64 to 512, as said below
Outputs:
- new_focusing: float32 [8, 512, 8192], P(('group', 'sub'), 'freq', 'recv'), parts along dimension 0
- new_residual: float32 [8, 512, 8192], P(('group', 'sub'), 'freq', 'recv'), parts along dimension 0
There are 2 independent parts, one for each index of `group`. A program takes and returns all parts, laid end to end along the dimension named above; each array names one. Nothing has to cross between parts.
Inputs may be any that keep to these rules, and one draw needn't show every extreme that they name: `window_end`: always above window_start.
All inputs are finite; a program needn't handle non-finite values.
Results may differ from a plain program's by a relative error of at most 0.005.
Values may be sent and summed in bfloat16 or wider, within the bound.
A program may use at most 192 MiB of HBM per device.

v0:
```python
import math

import jax
import jax.numpy as jnp
from jax import lax
from jax.sharding import PartitionSpec as P

NT = 512


first_bin = 4
relax_step = 1.0
highest = lax.Precision.HIGHEST


def dft_tables(count, samples):
    freqs = first_bin + jnp.arange(count, dtype=jnp.int32)
    sample_ids = jnp.arange(samples, dtype=jnp.int32)
    turns = (freqs[:, None] * sample_ids[None, :] % samples).astype(jnp.float32)
    phase = turns * (2.0 * math.pi / samples)
    weight = float(count * samples) ** (-0.25)
    return (jnp.cos(phase) * weight, jnp.sin(phase) * weight)


def spectrum_of(signal, cos_table, sin_table):
    real_part = jnp.einsum("ft,qtr->fqr", cos_table, signal, precision=highest)
    imag_part = -jnp.einsum("ft,qtr->fqr", sin_table, signal, precision=highest)
    return jnp.stack([real_part, imag_part]).astype(jnp.bfloat16)


def signal_of(spectrum, cos_table, sin_table):
    return jnp.einsum("ft,fqr->qtr", cos_table, spectrum[0], precision=highest) - jnp.einsum(
        "ft,fqr->qtr", sin_table, spectrum[1], precision=highest
    )


def contract(form, left, right):
    return jnp.einsum(form, left, right, preferred_element_type=jnp.float32)


def body(focusing, observed, recv_factor, source_factor, tile_ranks, window_start, window_end):
    freq_count = lax.axis_size("freq")
    recv_count = lax.axis_size("recv")
    sub_count = lax.axis_size("sub")
    bands = recv_factor.shape[1]
    rank_cols = recv_factor.shape[2]
    tiles_all = recv_factor.shape[3]
    tiles_here = source_factor.shape[3]
    half_foc, local_t, rec_block = focusing.shape
    tile_len = rec_block // tiles_here
    col_tiles = tiles_all // recv_count
    cos_table, sin_table = dft_tables(bands * freq_count, NT)
    rank_ids = lax.axis_index("sub") * rank_cols + jnp.arange(rank_cols, dtype=jnp.int32)
    rank_keep = (
        rank_ids[None, :, None, None] < jnp.transpose(tile_ranks, (0, 2, 1))[:, None, :, :]
    ).astype(jnp.float32)
    recv_tiles = recv_factor.reshape(2, bands, rank_cols, tiles_all, tiles_here, tile_len)
    recv_blocks = recv_factor.reshape(
        2, bands, rank_cols, recv_count, col_tiles, tiles_here, tile_len
    )
    source_blocks = source_factor.reshape(
        2, bands, rank_cols, tiles_here, recv_count, col_tiles, tile_len
    )
    keep_blocks = rank_keep.reshape(bands, rank_cols, recv_count, col_tiles, tiles_here)

    def forward(spec_half):
        gathered = lax.all_gather(spec_half, "sub", axis=2, tiled=True)
        tiles = gathered.reshape(2, bands, sub_count * half_foc, tiles_here, tile_len)
        real_part = contract("fkjin,fqin->fkjiq", recv_tiles[0], tiles[0]) - contract(
            "fkjin,fqin->fkjiq", recv_tiles[1], tiles[1]
        )
        imag_part = contract("fkjin,fqin->fkjiq", recv_tiles[0], tiles[1]) + contract(
            "fkjin,fqin->fkjiq", recv_tiles[1], tiles[0]
        )
        coeffs = (jnp.stack([real_part, imag_part]) * rank_keep[None, :, :, :, :, None]).astype(
            jnp.bfloat16
        )
        coeffs = coeffs.reshape(
            2, bands, rank_cols, recv_count, col_tiles, tiles_here, sub_count, half_foc
        )
        out_real = contract("fkibjn,fkbjiud->fbudjn", source_blocks[0], coeffs[0]) - contract(
            "fkibjn,fkbjiud->fbudjn", source_blocks[1], coeffs[1]
        )
        out_imag = contract("fkibjn,fkbjiud->fbudjn", source_blocks[0], coeffs[1]) + contract(
            "fkibjn,fkbjiud->fbudjn", source_blocks[1], coeffs[0]
        )
        partial_term = jnp.stack([out_real, out_imag]).reshape(
            2, bands, recv_count * sub_count * half_foc, rec_block
        )
        return lax.psum_scatter(partial_term, ("recv", "sub"), scatter_dimension=2, tiled=True)

    traces, seen = (focusing, observed)
    sample_ids = lax.axis_index("freq") * local_t + jnp.arange(local_t, dtype=jnp.int32)
    window = (
        (window_start[:, None, :] <= sample_ids[None, :, None])
        & (sample_ids[None, :, None] < window_end[:, None, :])
    ).astype(jnp.float32)

    def spectral(pieces):
        return lax.all_to_all(
            spectrum_of(pieces, cos_table, sin_table),
            "freq",
            split_axis=1,
            concat_axis=3,
            tiled=True,
        )

    def temporal(pieces):
        return lax.all_to_all(
            signal_of(pieces, cos_table, sin_table), "freq", split_axis=1, concat_axis=2, tiled=True
        )

    def to_spectrum(signal):
        return spectral(lax.all_to_all(signal, "freq", split_axis=2, concat_axis=1, tiled=True))

    def to_signal(spectrum):
        return temporal(lax.all_to_all(spectrum, "freq", split_axis=3, concat_axis=1, tiled=True))

    predicted = to_signal(forward(to_spectrum(traces)))
    residual = seen - window * predicted
    gathered = lax.all_gather(to_spectrum(window * residual), ("recv", "sub"), axis=2, tiled=True)
    tiles = gathered.reshape(2, bands, recv_count, sub_count, half_foc, col_tiles, tile_len)
    real_part = contract("fkibjn,fbudjn->fkbjiud", source_blocks[0], tiles[0]) + contract(
        "fkibjn,fbudjn->fkbjiud", source_blocks[1], tiles[1]
    )
    imag_part = contract("fkibjn,fbudjn->fkbjiud", source_blocks[0], tiles[1]) - contract(
        "fkibjn,fbudjn->fkbjiud", source_blocks[1], tiles[0]
    )
    coeffs = (
        jnp.stack([real_part, imag_part]) * keep_blocks[None, :, :, :, :, :, None, None]
    ).astype(jnp.bfloat16)
    out_real = contract("fkbjim,fkbjiud->fudim", recv_blocks[0], coeffs[0]) + contract(
        "fkbjim,fkbjiud->fudim", recv_blocks[1], coeffs[1]
    )
    out_imag = contract("fkbjim,fkbjiud->fudim", recv_blocks[0], coeffs[1]) - contract(
        "fkbjim,fkbjiud->fudim", recv_blocks[1], coeffs[0]
    )
    partial_term = jnp.stack([out_real, out_imag]).reshape(
        2, bands, sub_count * half_foc, rec_block
    )
    gradient = to_signal(lax.psum_scatter(partial_term, "sub", scatter_dimension=2, tiled=True))
    image = window * to_signal(forward(to_spectrum(gradient)))
    new_focus = traces + relax_step * gradient
    new_residual = residual - relax_step * image
    return (new_focus, new_residual)


def solution(mesh):
    placed = (
        P(("group", "sub"), "freq", "recv"),
        P(("group", "sub"), "freq", "recv"),
        P("group", "freq", "sub", None, "recv"),
        P("group", "freq", "sub", "recv", None),
        P(("group", "freq"), "recv", None),
        P(("group", "sub"), "recv"),
        P(("group", "sub"), "recv"),
    )
    return jax.shard_map(
        body,
        mesh=mesh,
        in_specs=placed,
        out_specs=(P(("group", "sub"), "freq", "recv"), P(("group", "sub"), "freq", "recv")),
        check_vma=False,
    )
```

profile of v0, /device:TPU:0, one launch (start us, length us, event | category | flops | bytes accessed | tf_op | source)
XLA Modules:
  0.0 1133.2 jit_solution(5497975495009939622)
XLA Ops:
  27.3 86.8 %all-to-all-done = f32[2,128,4096]{1,0,2:T(2,128)} async-done(((f32[2,128,4096]{1,0,2:T(2,128)}), f32[2,128,4096]{1,0,2:T(2,128)}, u32[]{:S(2)}, u32[]{:S(2)}) %all-to-all-start) | async-done | bytes 4194336 | tf_op jit(solution)/shard_map/all_to_all | solution.py:114
  169.1 32.3 %all-reduce.7.cloned.1.call-done = f32[2,1,8,4096]{3,2,1,0:T(8,128)} async-done(((f32[2,1,8,4096]{3,2,1,0:T(8,128)}), f32[2,1,8,4096]{3,2,1,0:T(8,128)}) %all-reduce.7.cloned.1.call-update) | async-done | bytes 262160
  202.4 18.3 %copy.179 = f32[2,1,2,4096]{2,1,0,3:T(1,128)} copy(f32[2,1,2,4096]{3,2,1,0:T(2,128)S(1)} %constant_dynamic-slice_fusion.2) | data formatting | bytes 131072 | tf_op jit(solution)/shard_map/reduce_scatter | solution.py:90
  221.2 16.3 %reduce.12 = f32[4096,2,2]{2,1,0:T(2,128)} reduce(f32[4096,2,1,2]{3,2,1,0:T(1,128)} %bitcast.415, f32[]{:T(128)} %broadcast.176), dimensions={2}, to_apply=%bitcast.364.reduce_sub_computation | reduce | bytes 131076
  245.1 10.1 all_to_all.207
  255.9 8.4 reshape.469
  302.3 79.7 %all-to-all-done.3 = f32[2,512,1024]{2,0,1:T(2,128)} async-done(((f32[2,512,1024]{2,0,1:T(2,128)}), f32[2,512,1024]{2,0,1:T(2,128)}, u32[]{:S(2)}, u32[]{:S(2)}) %all-to-all-start.3) | async-done | bytes 4194336 | tf_op jit(solution)/shard_map/all_to_all | solution.py:109
  382.0 9.1 copy.182
  391.2 13.9 %broadcast_select_fusion = f32[2,128,4096]{1,0,2:T(2,128)} fusion(f32[2,128,4096]{1,0,2:T(2,128)} %copy.183, f32[2,128,4,1024]{1,0,3,2:T(2,128)} %copy.182, s32[2,4096]{0,1:T(8,128)} %copy.155, s32[128]{0:T(128)S(1)} %iota_add_fusion.1, s32[2,4096]{0,1:T(8,128)} %copy.154), kind=kLoop, calls=%fused_computation.8 | loop fusion | flops 6291456 | bytes 12648960 | tf_op jit(solution)/shard_map/mul | solution.py:121
  410.1 92.6 %all-to-all-done.4 = f32[2,128,4096]{1,0,2:T(2,128)} async-done(((f32[2,128,4096]{1,0,2:T(2,128)}), f32[2,128,4096]{1,0,2:T(2,128)}, u32[]{:S(2)}, u32[]{:S(2)}) %all-to-all-start.4) | async-done | bytes 4194336 | tf_op jit(solution)/shard_map/all_to_all | solution.py:114
  557.2 14.5 %all-reduce.9.cloned.1.call-done = f32[2,1,4,4096]{3,2,1,0:T(4,128)} async-done(((f32[2,1,4,4096]{3,2,1,0:T(4,128)}), f32[2,1,4,4096]{3,2,1,0:T(4,128)}) %all-reduce.9.cloned.1.call-update) | async-done | bytes 131088
  579.1 16.3 %reduce.14 = f32[4096,2,2]{2,1,0:T(2,128)} reduce(f32[4096,2,1,2]{3,2,1,0:T(1,128)} %bitcast.417, f32[]{:T(128)} %broadcast.176), dimensions={2}, to_apply=%bitcast.366.reduce_sub_computation | reduce | bytes 131076
  603.0 10.6 all_to_all.208
  614.3 8.4 reshape.471
  644.1 98.4 %all_to_all.209 = f32[2,512,1024]{2,0,1:T(2,128)} all-to-all(f32[2,512,1024]{2,0,1:T(2,128)} %copy.209), channel_id=1, replica_groups=mesh['group'=2,'freq'=4,'recv'=2,'sub'=2] {'freq'}, dimensions={1} | all-to-all | bytes 8388608 | tf_op jit(solution)/shard_map/all_to_all | solution.py:109
  742.5 9.1 copy.210
  751.6 98.4 %all_to_all.210 = f32[2,128,4096]{1,0,2:T(2,128)} all-to-all(f32[2,128,4096]{1,0,2:T(2,128)} %bitcast.408), channel_id=1, replica_groups=mesh['group'=2,'freq'=4,'recv'=2,'sub'=2] {'freq'}, dimensions={2} | all-to-all | bytes 8388608 | tf_op jit(solution)/shard_map/all_to_all | solution.py:114
  897.2 30.4 %all-reduce.11.cloned.1.call-done = f32[2,1,8,4096]{3,2,1,0:T(8,128)} async-done(((f32[2,1,8,4096]{3,2,1,0:T(8,128)}), f32[2,1,8,4096]{3,2,1,0:T(8,128)}) %all-reduce.11.cloned.1.call-update) | async-done | bytes 262160
  935.4 16.3 %reduce.16 = f32[4096,2,2]{2,1,0:T(2,128)} reduce(f32[4096,2,1,2]{3,2,1,0:T(1,128)} %bitcast.420, f32[]{:T(128)} %broadcast.176), dimensions={2}, to_apply=%bitcast.368.reduce_sub_computation | reduce | bytes 131076
  959.2 10.3 all_to_all.212
  970.3 8.3 reshape.473
  1018.8 77.1 %all-to-all-done.11 = f32[2,512,1024]{2,0,1:T(2,128)} async-done(((f32[2,512,1024]{2,0,1:T(2,128)}), f32[2,512,1024]{2,0,1:T(2,128)}, u32[]{:S(2)}, u32[]{:S(2)}) %all-to-all-start.11) | async-done | bytes 4194336 | tf_op jit(solution)/shard_map/all_to_all | solution.py:109
  1095.9 9.2 copy.237
  1105.2 13.9 %fusion = f32[2,128,4096]{1,0,2:T(2,128)} fusion(f32[2,4,128,1024]{2,0,3,1:T(2,128)} %copy.237, f32[2,128,4096]{1,0,2:T(2,128)} %copy.183, f32[2,128,4,1024]{1,0,3,2:T(2,128)} %copy.182, s32[2,4096]{0,1:T(8,128)S(1)} %copy-done.6, s32[128]{0:T(128)S(1)} %iota_add_fusion.1, s32[2,4096]{0,1:T(8,128)} %copy.154), kind=kLoop, calls=%fused_computation.2 | loop fusion | flops 7340032 | bytes 16843264 | tf_op jit(solution)/shard_map/sub | solution.py:144
  (190 shorter events, 328.4 us)
Async XLA Ops:
  14.3 99.8 %all-to-all-start = ((f32[2,128,4096]{1,0,2:T(2,128)}), f32[2,128,4096]{1,0,2:T(2,128)}, u32[]{:S(2)}, u32[]{:S(2)}) async-start(f32[2,128,4096]{1,0,2:T(2,128)} %copy.211), calls=%async_computation | async-start | bytes 8388608 | tf_op jit(solution)/shard_map/all_to_all | solution.py:114
  20.7 4.2 copy-start.9
  121.3 4.5 copy-start.3
  125.8 6.2 copy-start.18
  128.7 12.5 %all-to-all-start.1 = ((bf16[2,4,2,1024]{3,2,0,1:T(2,128)(2,1)}), bf16[2,4,2,1024]{3,2,0,1:T(2,128)(2,1)S(1)}, u32[]{:S(2)}, u32[]{:S(2)}) async-start(bf16[2,4,2,1024]{3,2,0,1:T(2,128)(2,1)} %copy.158), calls=%async_computation.1 | async-start | bytes 65536 | tf_op jit(solution)/shard_map/all_to_all | solution.py:100
  132.0 69.4 %all-reduce.7.cloned.1.call-start = ((), (), s32[]{:S(2)}) async-start(), calls=%async_computation.12 | async-start | bytes 524288
  141.3 5.6 copy-start
  153.4 4.3 copy-start.13
  162.9 5.0 copy-start.20
  285.8 96.2 %all-to-all-start.3 = ((f32[2,512,1024]{2,0,1:T(2,128)}), f32[2,512,1024]{2,0,1:T(2,128)}, u32[]{:S(2)}, u32[]{:S(2)}) async-start(f32[2,512,1024]{2,0,1:T(2,128)} %copy.181), calls=%async_computation.3 | async-start | bytes 8388608 | tf_op jit(solution)/shard_map/all_to_all | solution.py:109
  291.1 7.2 copy-start.16
  405.1 97.6 %all-to-all-start.4 = ((f32[2,128,4096]{1,0,2:T(2,128)}), f32[2,128,4096]{1,0,2:T(2,128)}, u32[]{:S(2)}, u32[]{:S(2)}) async-start(f32[2,128,4096]{1,0,2:T(2,128)} %broadcast_select_fusion), calls=%async_computation.4 | async-start | bytes 8388608 | tf_op jit(solution)/shard_map/all_to_all | solution.py:114
  509.9 4.5 copy-start.4
  517.3 8.9 all-to-all-start.5
  520.6 51.1 %all-reduce.9.cloned.1.call-start = ((), (), s32[]{:S(2)}) async-start(), calls=%async_computation.13 | async-start | bytes 262144
  526.3 10.3 copy-start.11
  536.6 2.6 copy-start.14
  551.8 4.0 copy-start.19
  555.8 371.8 %all-reduce.11.cloned.1.call-start = ((), (), s32[]{:S(2)}) async-start(), calls=%async_computation.14 | async-start | bytes 524288
  857.2 4.5 copy-start.5
  872.3 5.4 copy-start.2
  886.3 4.9 copy-start.12
  1000.1 95.8 %all-to-all-start.11 = ((f32[2,512,1024]{2,0,1:T(2,128)}), f32[2,512,1024]{2,0,1:T(2,128)}, u32[]{:S(2)}, u32[]{:S(2)}) async-start(f32[2,512,1024]{2,0,1:T(2,128)} %copy.236), calls=%async_computation.11 | async-start | bytes 8388608 | tf_op jit(solution)/shard_map/all_to_all | solution.py:109
  1095.9 9.2 copy-start.6
  (6 other events, 11.3 us)
Sparse Core Ops, SparseCore 0:
  168.0 33.3 all-reduce.6
  555.9 15.6 all-reduce.8
  897.3 30.2 all-reduce.10
where the time goes:
time: 1140 us; the launch traced here: 1130 us
  waiting for transfers between devices  419 us (37%)
  blocking collectives  246 us (22%)
  local copies, waits for them, and re-layouts  228 us (20%)
  matrix products  107 us (9%)
  other arithmetic  89.1 us (8%)
  starting transfers between devices  28.1 us (2%)
  between operations  16 us (1%)
    all_to_all x2, waiting for transfers between devices, to_spectrum(): lax.all_to_all(signal, 'freq', split_axis=2, concat_axis=1, tiled=True)  179 us
    all_to_all x2, waiting for transfers between devices, temporal(): lax.all_to_all(signal_of(pieces, cos_table, sin_table), 'freq', split_axi...  157 us
    all_to_all x1, blocking collectives, to_spectrum(): lax.all_to_all(signal, 'freq', split_axis=2, concat_axis=1, tiled=True)  98.4 us
    all_to_all x1, blocking collectives, temporal(): lax.all_to_all(signal_of(pieces, cos_table, sin_table), 'freq', split_axi...  98.4 us
    unnamed x70, local copies, waits for them, and re-layouts  94.5 us
    unnamed x6, waiting for transfers between devices  77.3 us
    dot_general x24, matrix products, contract(): return jnp.einsum(form, left, right, preferred_element_type=jnp.float32)  60.6 us
    unnamed x3, other arithmetic  48.9 us
  transfers between devices with their start and end apart: 9, of which 8 were waited for; matrix products, arithmetic and copies ran while one was open for 4% of the time, Pallas kernels for 0%

commit v1 on v0

--- a/solution.py
+++ b/solution.py
@@ -20,12 +20,6 @@
     phase = turns * (2.0 * math.pi / samples)
     weight = float(count * samples) ** (-0.25)
     return (jnp.cos(phase) * weight, jnp.sin(phase) * weight)
-
-
-def spectrum_of(signal, cos_table, sin_table):
-    real_part = jnp.einsum("ft,qtr->fqr", cos_table, signal, precision=highest)
-    imag_part = -jnp.einsum("ft,qtr->fqr", sin_table, signal, precision=highest)
-    return jnp.stack([real_part, imag_part]).astype(jnp.bfloat16)
 
 
 def signal_of(spectrum, cos_table, sin_table):
@@ -96,25 +90,21 @@
         & (sample_ids[None, :, None] < window_end[:, None, :])
     ).astype(jnp.float32)
 
-    def spectral(pieces):
-        return lax.all_to_all(
-            spectrum_of(pieces, cos_table, sin_table),
-            "freq",
-            split_axis=1,
-            concat_axis=3,
-            tiled=True,
-        )
-
-    def temporal(pieces):
-        return lax.all_to_all(
-            signal_of(pieces, cos_table, sin_table), "freq", split_axis=1, concat_axis=2, tiled=True
-        )
+    local_cos = lax.dynamic_slice_in_dim(cos_table, lax.axis_index("freq") * local_t, local_t, 1)
+    local_sin = lax.dynamic_slice_in_dim(sin_table, lax.axis_index("freq") * local_t, local_t, 1)
 
     def to_spectrum(signal):
-        return spectral(lax.all_to_all(signal, "freq", split_axis=2, concat_axis=1, tiled=True))
+        real_part = jnp.einsum("ft,qtr->fqr", local_cos, signal, precision=highest)
+        imag_part = -jnp.einsum("ft,qtr->fqr", local_sin, signal, precision=highest)
+        whole = lax.psum_scatter(
+            jnp.stack([real_part, imag_part]), "freq", scatter_dimension=1, tiled=True
+        )
+        return whole.astype(jnp.bfloat16)
 
     def to_signal(spectrum):
-        return temporal(lax.all_to_all(spectrum, "freq", split_axis=3, concat_axis=1, tiled=True))
+        return signal_of(
+            lax.all_gather(spectrum, "freq", axis=1, tiled=True), local_cos, local_sin
+        )
 
     predicted = to_signal(forward(to_spectrum(traces)))
     residual = seen - window * predicted
@@ -138,8 +128,10 @@
     partial_term = jnp.stack([out_real, out_imag]).reshape(
         2, bands, sub_count * half_foc, rec_block
     )
-    gradient = to_signal(lax.psum_scatter(partial_term, "sub", scatter_dimension=2, tiled=True))
-    image = window * to_signal(forward(to_spectrum(gradient)))
+    grad_spec = lax.psum_scatter(partial_term, "sub", scatter_dimension=2, tiled=True)
+    gradient = to_signal(grad_spec)
+    gain = (0.5 * NT) * float(bands * freq_count * NT) ** (-0.5)
+    image = window * to_signal(forward((grad_spec * gain).astype(jnp.bfloat16)))
     new_focus = traces + relax_step * gradient
     new_residual = residual - relax_step * image
     return (new_focus, new_residual)

time: 1140 us -> 329 us (0.29)
  waiting for transfers between devices: 419 us -> 32.7 us
  local copies, waits for them, and re-layouts: 228 us -> 49.9 us
  blocking collectives: 246 us -> 102 us
  other arithmetic: 89.1 us -> 2.49 us
  starting transfers between devices: 28.1 us -> 0.12 us
  matrix products: 107 us -> 121 us
    all_to_all x6 -> x0, waiting for transfers between devices: 342 us -> none  [the longest x2 179 us: to_spectrum(): lax.all_to_all(signal, 'freq', split_axis=2, concat_axis=1, tiled=True)]
    all_to_all x6 -> x0, blocking collectives: 236 us -> none  [the longest x1 98.4 us: to_spectrum(): lax.all_to_all(signal, 'freq', split_axis=2, concat_axis=1, tiled=True)]
    all_to_all x15 -> x0, local copies, waits for them, and re-layouts: 64.9 us -> none  [the longest x3 27.5 us: temporal(): lax.all_to_all(signal_of(pieces, cos_table, sin_table), 'freq', split_axi...]
    unnamed x70 -> x59, local copies, waits for them, and re-layouts: 94.5 us -> 31.7 us
    unnamed x0 -> x2, blocking collectives: none -> 48.9 us
    unnamed x3 -> x0, other arithmetic: 48.9 us -> none
    unnamed x6, waiting for transfers between devices: 77.3 us -> 32.7 us
    all_gather x0 -> x3, blocking collectives: none -> 43.4 us  [to_signal(): lax.all_gather(spectrum, 'freq', axis=1, tiled=True)]
  transfers between devices with their start and end apart: 9 -> 3, of which waited for: 8 -> 2; matrix products, arithmetic and copies ran while one was open for 4% -> 10% of each run, Pallas kernels for 0% -> 0%
where the time goes in v1:
time: 329 us; the launch traced here: 324 us
  matrix products  121 us (37%)
  blocking collectives  102 us (31%)
  local copies, waits for them, and re-layouts  49.9 us (15%)
  waiting for transfers between devices  32.7 us (10%)
  between operations  15.8 us (5%)
    dot_general x24, matrix products, contract(): return jnp.einsum(form, left, right, preferred_element_type=jnp.float32)  56 us
    unnamed x2, blocking collectives  48.9 us
    all_gather x3, blocking collectives, to_signal(): lax.all_gather(spectrum, 'freq', axis=1, tiled=True)  43.4 us
    unnamed x6, waiting for transfers between devices  32.7 us
    unnamed x59, local copies, waits for them, and re-layouts  31.7 us
    dot_general x3, matrix products, signal_of(): jnp.einsum('ft,fqr->qtr', sin_table, spectrum[1], precision=highest)  27.7 us
    dot_general x3, matrix products, signal_of(): jnp.einsum('ft,fqr->qtr', cos_table, spectrum[0], precision=highest)  20.1 us
    dot_general x2, matrix products, to_spectrum(): real_part = jnp.einsum('ft,qtr->fqr', local_cos, signal, precision=highest)  9.69 us
  transfers between devices with their start and end apart: 3, of which 2 were waited for; matrix products, arithmetic and copies ran while one was open for 10% of the time, Pallas kernels for 0%

profile of v1, /device:TPU:0, one launch (start us, length us, event | category | flops | bytes accessed | tf_op | source)
XLA Modules:
  0.0 324.1 jit_solution(17048973335724173983)
XLA Ops:
  7.3 4.4 %convolution_bitcast_fusion.1 = f32[1,4,2,4096]{3,1,2,0:T(4,128)S(1)} fusion(f32[2,128,4096]{2,1,0:T(8,128)} %param.7, f32[4,512]{1,0:T(4,128)S(1)} %fusion.130, s32[]{:T(128)S(6)} %select_n.14), kind=kOutput, calls=%fused_computation.16 | convolution fusion | flops 50332160 | bytes 4327428 | tf_op jit(solution)/shard_map/ft,qtr->fqr/dot_general | solution.py:97
  14.1 25.9 %all-reduce.16 = bf16[2,4,2,4096]{3,2,0,1:T(2,128)(2,1)S(1)} all-reduce(f32[2,4,2,4096]{3,2,0,1:T(2,128)S(1)} %copy.182), channel_id=2, replica_groups=mesh['group'=2,'freq'=4,'recv'=2,'sub'=2] {'freq'}, use_global_device_ids=true, to_apply=%region_0.1.clone | all-reduce | flops 65536 | bytes 393216
  72.3 4.2 %fusion.67 = f32[1,2,2,2,16,256]{5,3,2,4,1,0:T(2,128)S(1)} fusion(f32[2,16,2,2,256]{4,3,2,1,0:T(2,128)S(1)} %convolution_bitcast_fusion.6, bf16[8,2,16,16,2,2]{3,5,0,4,2,1:T(2,128)(2,1)S(1)} %copy.194, bf16[8,16,2,16,256,1]{4,3,2,1,0,5:T(8,128)(2,1)} %bitcast.344), kind=kOutput, calls=%fused_computation.69 | convolution fusion | flops 8421376 | bytes 2392064 | tf_op jit(solution)/shard_map/fkibjn,fkbjiud->fbudjn/dot_general | solution.py:32
  78.4 5.6 %copy.206 = f32[2,128,4096]{1,2,0:T(8,128)} copy(f32[2,128,4096]{2,1,0:T(8,128)} %param.8) | data formatting | bytes 8388608 | tf_op args[1]
  84.7 23.6 %all-reduce.11.cloned.1.call-done = f32[2,1,8,4096]{3,0,1,2:T(2,128)} async-done(((f32[2,1,8,4096]{3,0,1,2:T(2,128)}), f32[2,1,8,4096]{3,0,1,2:T(2,128)}) %all-reduce.11.cloned.1.call-update) | async-done | bytes 262160
  109.2 14.1 %all_gather.19 = f32[2,4,2,4096]{3,2,0,1:T(2,128)S(1)} all-gather(f32[2,1,2,4096]{3,2,0,1:T(2,128)S(1)} %copy.203), channel_id=1, replica_groups=mesh['group'=2,'freq'=4,'recv'=2,'sub'=2] {'freq'}, dimensions={1}, use_global_device_ids=true | all-gather | bytes 327680 | tf_op jit(solution)/shard_map/all_gather | solution.py:106
  123.3 6.7 %fusion.115 = f32[2,4096,128]{2,1,0:T(8,128)S(1)} fusion(f32[1,4,2,4096]{3,2,0,1:T(2,128)S(1)} %get-tuple-element.31, f32[4,512]{1,0:T(4,128)S(1)} %fusion.130, s32[]{:T(128)S(6)} %select_n.14), kind=kOutput, calls=%fused_computation.119 | convolution fusion | flops 50332160 | bytes 4327428 | tf_op jit(solution)/shard_map/ft,fqr->qtr/dot_general | solution.py:26
  130.0 9.0 %fusion.7 = f32[2,128,4096]{1,2,0:T(8,128)S(1)} fusion(f32[2,128,4096]{1,2,0:T(8,128)S(1)} %copy-done.6, f32[2,4096,128]{2,1,0:T(8,128)S(1)} %fusion.115, f32[1,4,2,4096]{3,2,0,1:T(2,128)S(1)} %get-tuple-element.30, f32[4,512]{1,0:T(4,128)S(1)} %fusion.130, s32[]{:T(128)S(6)} %select_n.14, s32[2,4096]{1,0:T(2,128)S(1)} %copy-done.14, ...), kind=kOutput, calls=%fused_computation.10 | convolution fusion | flops 56623616 | bytes 12782084 | tf_op jit(solution)/shard_map/ft,fqr->qtr/dot_general | solution.py:26
  139.1 5.3 %convolution_bitcast_fusion = f32[1,4,2,4096]{3,1,2,0:T(4,128)S(1)} fusion(f32[2,128,4096]{1,2,0:T(8,128)S(1)} %fusion.7, f32[4,512]{1,0:T(4,128)S(1)} %fusion.130, s32[]{:T(128)S(6)} %select_n.14, s32[2,4096]{1,0:T(2,128)S(1)} %copy-done.14, s32[128]{0:T(128)S(1)} %iota_add_fusion.1, s32[2,4096]{1,0:T(2,128)S(1)} %copy-done.15), kind=kOutput, calls=%fused_computation.13 | convolution fusion | flops 54526464 | bytes 4393476 | tf_op jit(solution)/shard_map/ft,qtr->fqr/dot_general | solution.py:97
  144.3 5.3 %fusion.8 = f32[1,4,2,4096]{3,1,2,0:T(4,128)S(1)} fusion(f32[2,128,4096]{1,2,0:T(8,128)S(1)} %fusion.7, f32[4,512]{1,0:T(4,128)S(1)} %fusion.130, s32[]{:T(128)S(6)} %select_n.14, s32[2,4096]{1,0:T(2,128)S(1)} %copy-done.14, s32[128]{0:T(128)S(1)} %iota_add_fusion.1, s32[2,4096]{1,0:T(2,128)S(1)} %copy-done.15), kind=kOutput, calls=%fused_computation.12 | convolution fusion | flops 54559232 | bytes 4393476 | tf_op jit(solution)/shard_map/ft,qtr->fqr/dot_general | solution.py:98
  149.9 23.1 %all-reduce.17 = bf16[2,4,2,4096]{3,2,0,1:T(2,128)(2,1)S(1)} all-reduce(f32[2,4,2,4096]{3,2,0,1:T(2,128)S(1)} %copy.209), channel_id=4, replica_groups=mesh['group'=2,'freq'=4,'recv'=2,'sub'=2] {'freq'}, use_global_device_ids=true, to_apply=%region_2.3.clone | all-reduce | flops 65536 | bytes 393216
  173.8 5.8 %all_gather.20 = bf16[2,1,8,4096]{3,0,1,2:T(2,128)(2,1)S(1)} all-gather(bf16[2,1,2,4096]{3,0,1,2:T(2,128)(2,1)S(1)} %copy.210), channel_id=1, replica_groups=mesh['group'=2,'freq'=4,'recv'=2,'sub'=2] {'recv','sub'}, dimensions={2}, use_global_device_ids=true | all-gather | bytes 163840 | tf_op jit(solution)/shard_map/all_gather | solution.py:111
  180.3 4.2 %fusion.107 = f32[2,16,2,2,8,16]{5,3,4,2,1,0:T(2,128)S(1)} fusion(bf16[8,16,2,16,256,1]{4,3,2,1,0,5:T(8,128)(2,1)} %bitcast.345, bf16[2,2,2,16,256,1]{4,3,2,1,0,5:T(8,128)(2,1)S(1)} %bitcast.370), kind=kOutput, calls=%fused_computation.94 | convolution fusion | flops 8388608 | bytes 2228224 | tf_op jit(solution)/shard_map/fkibjn,fbudjn->fkbjiud/dot_general | solution.py:32
  204.0 5.6 %copy.234 = f32[2,128,4096]{1,2,0:T(8,128)} copy(f32[2,128,4096]{2,1,0:T(8,128)} %param.7) | data formatting | bytes 8388608 | tf_op args[0]
  210.7 9.0 %all-reduce.13.cloned.1.call-done = f32[2,1,4,4096]{3,0,1,2:T(2,128)} async-done(((f32[2,1,4,4096]{3,0,1,2:T(2,128)}), f32[2,1,4,4096]{3,0,1,2:T(2,128)}) %all-reduce.13.cloned.1.call-update) | async-done | bytes 131088
  233.3 4.1 %convolution_bitcast_fusion.2 = f32[2,16,2,2,256]{4,3,2,1,0:T(2,128)S(1)} fusion(bf16[8,2,16,16,2,2]{3,5,0,4,2,1:T(2,128)(2,1)S(1)} %copy.243, bf16[8,16,2,16,256,1]{4,3,2,1,0,5:T(8,128)(2,1)} %bitcast.349), kind=kOutput, calls=%fused_computation.58 | convolution fusion | flops 8388608 | bytes 2260992 | tf_op jit(solution)/shard_map/fkibjn,fkbjiud->fbudjn/dot_general | solution.py:32
  243.8 14.6 %all_gather.21 = f32[2,4,2,4096]{3,2,0,1:T(2,128)S(1)} all-gather(f32[2,1,2,4096]{3,2,0,1:T(2,128)S(1)} %copy.231), channel_id=1, replica_groups=mesh['group'=2,'freq'=4,'recv'=2,'sub'=2] {'freq'}, dimensions={1}, use_global_device_ids=true | all-gather | bytes 327680 | tf_op jit(solution)/shard_map/all_gather | solution.py:106
  258.4 6.7 %fusion.114 = f32[2,4096,128]{2,1,0:T(8,128)S(1)} fusion(f32[1,4,2,4096]{3,2,0,1:T(2,128)S(1)} %get-tuple-element.29, f32[4,512]{1,0:T(4,128)S(1)} %fusion.130, s32[]{:T(128)S(6)} %select_n.14), kind=kOutput, calls=%fused_computation.116 | convolution fusion | flops 50332160 | bytes 4327428 | tf_op jit(solution)/shard_map/ft,fqr->qtr/dot_general | solution.py:26
  265.1 8.4 %fusion.4 = f32[2,128,4096]{1,2,0:T(8,128)} fusion(f32[2,128,4096]{1,2,0:T(8,128)S(1)} %copy-done.7, f32[2,4096,128]{2,1,0:T(8,128)S(1)} %fusion.114, f32[1,4,2,4096]{3,2,0,1:T(2,128)S(1)} %get-tuple-element.28, f32[4,512]{1,0:T(4,128)S(1)} %fusion.130, s32[]{:T(128)S(6)} %select_n.14), kind=kOutput, calls=%fused_computation.6 | convolution fusion | flops 52429312 | bytes 12716036 | tf_op jit(solution)/shard_map/ft,fqr->qtr/dot_general | solution.py:26
  273.5 5.6 %copy.257 = f32[2,128,4096]{2,1,0:T(8,128)} copy(f32[2,128,4096]{1,2,0:T(8,128)} %fusion.4) | data formatting | bytes 8388608
  280.0 14.7 %all_gather.23 = f32[2,4,2,4096]{3,2,0,1:T(2,128)S(1)} all-gather(f32[2,1,2,4096]{3,2,0,1:T(2,128)S(1)} %copy.254), channel_id=1, replica_groups=mesh['group'=2,'freq'=4,'recv'=2,'sub'=2] {'freq'}, dimensions={1}, use_global_device_ids=true | all-gather | bytes 327680 | tf_op jit(solution)/shard_map/all_gather | solution.py:106
  294.7 6.7 %fusion.113 = f32[2,4096,128]{2,1,0:T(8,128)S(1)} fusion(f32[1,4,2,4096]{3,2,0,1:T(2,128)S(1)} %get-tuple-element.25, f32[4,512]{1,0:T(4,128)S(1)} %fusion.130, s32[]{:T(128)S(6)} %select_n.14), kind=kOutput, calls=%fused_computation.113 | convolution fusion | flops 50332160 | bytes 4327428 | tf_op jit(solution)/shard_map/ft,fqr->qtr/dot_general | solution.py:26
  301.5 10.3 %fusion.2 = f32[2,128,4096]{1,2,0:T(8,128)} fusion(f32[2,128,4096]{1,2,0:T(8,128)S(1)} %copy-done.5, f32[2,4096,128]{2,1,0:T(8,128)S(1)} %fusion.113, f32[1,4,2,4096]{3,2,0,1:T(2,128)S(1)} %get-tuple-element.24, f32[4,512]{1,0:T(4,128)S(1)} %fusion.130, s32[]{:T(128)S(6)} %select_n.14, s32[2,4096]{1,0:T(2,128)S(1)} %copy-done.14, ...), kind=kOutput, calls=%fused_computation.3 | convolution fusion | flops 56623616 | bytes 12782084 | tf_op jit(solution)/shard_map/ft,fqr->qtr/dot_general | solution.py:26
  311.8 5.6 %copy.258 = f32[2,128,4096]{2,1,0:T(8,128)} copy(f32[2,128,4096]{1,2,0:T(8,128)} %fusion.2) | data formatting | bytes 8388608
  (147 shorter events, 79.8 us)
Async XLA Ops:
  7.2 101.1 %all-reduce.11.cloned.1.call-start = ((), (), s32[]{:S(2)}) async-start(), calls=%async_computation | async-start | bytes 524288
  7.3 4.4 %copy-start.3 = (f32[2,128,4096]{2,1,0:T(8,128)S(1)}, f32[2,128,4096]{2,1,0:T(8,128)}, u32[]{:S(2)}) copy-start(f32[2,128,4096]{2,1,0:T(8,128)} %param.7) | copy-start | bytes 12582916
  11.8 28.3 %copy-start.19 = (u32[32]{0:T(128)S(1)}, u32[32]{0:T(128)}, u32[]{:S(2)}) copy-start(u32[32]{0:T(128)} %constant.50) | copy-start | bytes 388
  47.8 4.5 %copy-start = (bf16[32,8,16,256]{3,2,1,0:T(8,128)(2,1)}, bf16[32,8,16,256]{3,2,1,0:T(8,128)(2,1)S(1)}, u32[]{:S(2)}) copy-start(bf16[32,8,16,256]{3,2,1,0:T(8,128)(2,1)S(1)} %copy.365) | copy-start | bytes 6291460
  50.8 3.0 copy-start.16
  62.0 2.4 copy-start.11
  64.4 5.2 %copy-start.8 = (bf16[16,8,32,256]{3,2,1,0:T(8,128)(2,1)}, bf16[16,8,32,256]{3,2,1,0:T(8,128)(2,1)S(1)}, u32[]{:S(2)}) copy-start(bf16[16,8,32,256]{3,2,1,0:T(8,128)(2,1)S(1)} %copy.368) | copy-start | bytes 6291460
  72.3 5.4 %copy-start.18 = (u32[32]{0:T(128)S(1)}, u32[32]{0:T(128)}, u32[]{:S(2)}) copy-start(u32[32]{0:T(128)} %constant.54) | copy-start | bytes 388
  77.6 142.2 %all-reduce.13.cloned.1.call-start = ((), (), s32[]{:S(2)}) async-start(), calls=%async_computation.1 | async-start | bytes 262144
  123.3 6.7 %copy-start.6 = (f32[2,128,4096]{1,2,0:T(8,128)S(1)}, f32[2,128,4096]{1,2,0:T(8,128)}, u32[]{:S(2)}) copy-start(f32[2,128,4096]{1,2,0:T(8,128)} %copy.206) | copy-start | bytes 12582916
  123.3 6.7 %copy-start.14 = (s32[2,4096]{1,0:T(2,128)S(1)}, s32[2,4096]{1,0:T(2,128)}, u32[]{:S(2)}) copy-start(s32[2,4096]{1,0:T(2,128)} %param.13) | copy-start | bytes 98308
  123.3 6.7 %copy-start.15 = (s32[2,4096]{1,0:T(2,128)S(1)}, s32[2,4096]{1,0:T(2,128)}, u32[]{:S(2)}) copy-start(s32[2,4096]{1,0:T(2,128)} %param.12) | copy-start | bytes 98308
  139.1 5.3 %copy-start.4 = (f32[2,128,4096]{1,2,0:T(8,128)}, f32[2,128,4096]{1,2,0:T(8,128)S(1)}, u32[]{:S(2)}) copy-start(f32[2,128,4096]{1,2,0:T(8,128)S(1)} %fusion.7) | copy-start | bytes 12582916
  173.0 11.5 %copy-start.9 = (bf16[16,8,32,256]{3,2,1,0:T(8,128)(2,1)S(1)}, bf16[16,8,32,256]{3,2,1,0:T(8,128)(2,1)}, u32[]{:S(2)}) copy-start(bf16[16,8,32,256]{3,2,1,0:T(8,128)(2,1)} %copy-done.8) | copy-start | bytes 6291460
  184.4 2.6 copy-start.12
  194.8 3.3 %copy-start.1 = (bf16[32,8,16,256]{3,2,1,0:T(8,128)(2,1)S(1)}, bf16[32,8,16,256]{3,2,1,0:T(8,128)(2,1)}, u32[]{:S(2)}) copy-start(bf16[32,8,16,256]{3,2,1,0:T(8,128)(2,1)} %copy-done) | copy-start | bytes 6291460
  203.9 5.7 %copy-start.17 = (u32[32]{0:T(128)S(1)}, u32[32]{0:T(128)}, u32[]{:S(2)}) copy-start(u32[32]{0:T(128)} %constant.62) | copy-start | bytes 388
  203.9 75.2 %all-reduce.15.cloned.1.call-start = ((), (), s32[]{:S(2)}) async-start(), calls=%async_computation.2 | async-start | bytes 524288
  222.8 3.0 copy-start.2
  227.3 2.7 copy-start.13
  232.5 4.9 %copy-start.10 = (bf16[16,8,32,256]{3,2,1,0:T(8,128)(2,1)S(1)}, bf16[16,8,32,256]{3,2,1,0:T(8,128)(2,1)}, u32[]{:S(2)}) copy-start(bf16[16,8,32,256]{3,2,1,0:T(8,128)(2,1)} %copy-done.8) | copy-start | bytes 6291460
  258.4 6.7 %copy-start.7 = (f32[2,128,4096]{1,2,0:T(8,128)S(1)}, f32[2,128,4096]{1,2,0:T(8,128)}, u32[]{:S(2)}) copy-start(f32[2,128,4096]{1,2,0:T(8,128)} %copy.234) | copy-start | bytes 12582916
  294.7 6.7 %copy-start.5 = (f32[2,128,4096]{1,2,0:T(8,128)S(1)}, f32[2,128,4096]{1,2,0:T(8,128)}, u32[]{:S(2)}) copy-start(f32[2,128,4096]{1,2,0:T(8,128)} %copy-done.4) | copy-start | bytes 12582916
Sparse Core Ops, SparseCore 0:
  77.7 30.5 all-reduce.10
  204.0 15.6 all-reduce.12
  243.8 33.1 all-reduce.14

commit v2 on v1

--- a/solution.py
+++ b/solution.py
@@ -1,8 +1,11 @@
+import functools
 import math
 
 import jax
 import jax.numpy as jnp
 from jax import lax
+from jax.experimental import pallas as pl
+from jax.experimental.pallas import tpu as pltpu
 from jax.sharding import PartitionSpec as P
 
 NT = 512
@@ -137,6 +140,334 @@
     return (new_focus, new_residual)
 
 
+CHUNK = 512
+
+
+def dot(a, b):
+    return lax.dot_general(a, b, (((1,), (0,)), ((), ())), preferred_element_type=jnp.float32)
+
+
+def dot_nt(a, b):
+    return lax.dot_general(a, b, (((1,), (1,)), ((), ())), preferred_element_type=jnp.float32)
+
+
+def turned(x, sign):
+    row = lax.broadcasted_iota(jnp.int32, x.shape, 0)
+    up = pltpu.roll(x, x.shape[0] - 1, 0)
+    down = pltpu.roll(x, 1, 0)
+    return jnp.where(row % 2 == 0, -sign * up, sign * down)
+
+
+def halves(x):
+    high = x.astype(jnp.bfloat16)
+    return high, (x - high.astype(jnp.float32)).astype(jnp.bfloat16)
+
+
+def spectrum_chunk(table_wide, v):
+    out = dot(table_wide, jnp.concatenate(halves(v), axis=0))
+    rows = out.shape[0] // 2
+    return out[:rows] + out[rows:]
+
+
+def signal_chunk(table_tall, p):
+    high, low = halves(p)
+    high, low = high.astype(jnp.float32), low.astype(jnp.float32)
+    return dot(table_tall, jnp.concatenate([high, low, high, low], axis=0).astype(jnp.bfloat16))
+
+
+def seen_rows(ref, d, lanes, count):
+    return jnp.concatenate([ref[f, 2 * d : 2 * d + 2, lanes] for f in range(count)], axis=0)
+
+
+def core_kernel(
+    nf, tiles, tiles_here, ranks, tile_len, gain,
+    foc, obs, uf, vf, keep_f, keep_a, start, end, tids, table_wide, table_tall,
+    p_out, g_out,
+    sp, zrecv, zsum, zother, coef, ybuf, yrecv, pg, zg, adj, ga, gother, gg,
+    send_sem, recv_sem,
+):
+    z, x, c = lax.axis_index("freq"), lax.axis_index("recv"), lax.axis_index("sub")
+    lanes_all = tiles_here * tile_len
+    peers = [(dx, dc) for dx in range(2) for dc in range(2) if dx + dc]
+    zs = [{"freq": lax.rem(z + k, nf)} for k in range(1, nf)]
+    near = [{"recv": x + dx - 2 * dx * x, "sub": c + dc - 2 * dc * c} for dx, dc in peers]
+    barrier = pltpu.get_barrier_semaphore()
+    for device in zs + near:
+        pl.semaphore_signal(
+            barrier, inc=1, device_id=device, device_id_type=pl.DeviceIdType.MESH
+        )
+    pl.semaphore_wait(barrier, nf - 1 + len(peers))
+    used = [0]
+
+    def send(src, dst, device):
+        n = used[0]
+        used[0] += 1
+        copy = pltpu.make_async_remote_copy(
+            src_ref=src, dst_ref=dst, send_sem=send_sem.at[n], recv_sem=recv_sem.at[n],
+            device_id=device, device_id_type=pl.DeviceIdType.MESH,
+        )
+        copy.start()
+        return copy
+
+    def reduce_freq(n):
+        copies = [
+            send(sp.at[n, zs[k]["freq"]], zrecv.at[n, k], zs[k]) for k in range(nf - 1)
+        ]
+        for copy in copies:
+            copy.wait()
+        total = sp[n, z]
+        for k in range(nf - 1):
+            total = total + zrecv[n, k]
+        return total
+
+    def gather_freq(buf):
+        return [send(buf.at[z], buf.at[z], zs[k]) for k in range(nf - 1)]
+
+    def put_spectrum(n, d, lanes, out):
+        for f in range(nf):
+            sp[n, f, 2 * d : 2 * d + 2, lanes] = out[2 * f : 2 * f + 2]
+
+    def forward(n, get):
+        def first(i, carry):
+            lanes = pl.ds(pl.multiple_of(i * tile_len, tile_len), tile_len)
+            out = dot_nt(get(lanes).astype(jnp.bfloat16), uf[:, lanes])
+            half = out.shape[1] // 2
+            coef[pl.ds(pl.multiple_of(i * 8, 8), 8), :] = out[:, :half] + turned(out[:, half:], 1.0)
+            return carry
+
+        lax.fori_loop(0, tiles_here, first, 0)
+        kept = (coef[...] * keep_f[...]).astype(jnp.bfloat16)
+        kj, ki = ranks * tiles, ranks * tiles_here
+        row = lax.broadcasted_iota(jnp.int32, (kj, 2 * ki), 0)
+        col = lax.broadcasted_iota(jnp.int32, (kj, 2 * ki), 1)
+        same_k = row // tiles == (col % ki) // tiles_here
+        shift = row % tiles - col // ki
+        row_i = lax.broadcasted_iota(jnp.int32, (8 * tiles_here, 2 * ki), 0) // 8
+        col_i = lax.broadcasted_iota(jnp.int32, (8 * tiles_here, 2 * ki), 1) % tiles_here
+        own = row_i == col_i
+
+        def second(jp, carry):
+            pick = jnp.where(same_k & (shift == 2 * jp), 1.0, 0.0).astype(jnp.bfloat16)
+            wide = jnp.where(own, dot(kept, pick), 0.0)
+            both = jnp.sum(wide.reshape(tiles_here, 8, 2 * ki), axis=0)
+            for jj in range(2):
+                part = both[:, jj * ki : (jj + 1) * ki]
+                lhs = jnp.concatenate([part, turned(part, 1.0)], axis=1).astype(jnp.bfloat16)
+                at = pl.multiple_of((2 * jp + jj) * tile_len, tile_len)
+                out = dot(lhs, vf[:, pl.ds(at, tile_len)])
+                block = jp // (tiles_here // 2)
+                at = pl.multiple_of((2 * jp + jj - block * tiles_here) * tile_len, tile_len)
+                ybuf[n, block, 0, :, pl.ds(at, tile_len)] = out[:4]
+                ybuf[n, block, 1, :, pl.ds(at, tile_len)] = out[4:]
+            return carry
+
+        lax.fori_loop(0, tiles // 2, second, 0)
+        copies = [
+            send(ybuf.at[n, device["recv"], device["sub"]], yrecv.at[n, k], device)
+            for k, device in enumerate(near)
+        ]
+        for copy in copies:
+            copy.wait()
+        total = ybuf[n, x, c]
+        for k in range(len(near)):
+            total = total + yrecv[n, k]
+        pg[n, z] = total
+        for copy in gather_freq(pg.at[n]):
+            copy.wait()
+
+    def chunks(step):
+        def one(k, carry):
+            step(pl.ds(pl.multiple_of(k * CHUNK, CHUNK), CHUNK))
+            return carry
+
+        lax.fori_loop(0, lanes_all // CHUNK, one, 0)
+
+    def start_spec(lanes):
+        for d in range(2):
+            put_spectrum(0, d, lanes, spectrum_chunk(table_wide[...], foc[d, :, lanes]))
+
+    chunks(start_spec)
+    zsum[...] = reduce_freq(0)
+    send(zsum, zother, {"sub": 1 - c}).wait()
+
+    def spec_rows(lanes):
+        mine, other = zsum[:, lanes], zother[:, lanes]
+        first, last = jnp.where(c == 0, mine, other), jnp.where(c == 0, other, mine)
+        return jnp.concatenate([first, last], axis=0)
+
+    forward(0, spec_rows)
+
+    def windowed(lanes):
+        for d in range(2):
+            signal = signal_chunk(table_tall[...], seen_rows(pg.at[0], d, lanes, nf))
+            t = tids[...]
+            inside = (start[d : d + 1, lanes] <= t) & (t < end[d : d + 1, lanes])
+            kept = jnp.where(inside, obs[d, :, lanes] - signal, 0.0)
+            put_spectrum(1, d, lanes, spectrum_chunk(table_wide[...], kept))
+
+    chunks(windowed)
+    zg[x, c] = reduce_freq(1)
+    for copy in [send(zg.at[x, c], zg.at[x, c], device) for device in near]:
+        copy.wait()
+
+    ki, kj = ranks * tiles_here, ranks * tiles
+
+    def adjoint_first(j, carry):
+        block = j // tiles_here
+        at = pl.multiple_of((j - block * tiles_here) * tile_len, tile_len)
+        rows = jnp.concatenate(
+            [zg[block, 0, :, pl.ds(at, tile_len)], zg[block, 1, :, pl.ds(at, tile_len)]], axis=0
+        )
+        at = pl.multiple_of(j * tile_len, tile_len)
+        out = dot_nt(rows.astype(jnp.bfloat16), vf[:, pl.ds(at, tile_len)])
+        adj[pl.ds(pl.multiple_of(j * 8, 8), 8), :] = out[:, :ki] + turned(out[:, ki:], -1.0)
+        return carry
+
+    lax.fori_loop(0, tiles, adjoint_first, 0)
+    kept_a = (adj[...] * keep_a[...]).astype(jnp.bfloat16)
+    row = lax.broadcasted_iota(jnp.int32, (ki, kj), 0)
+    col = lax.broadcasted_iota(jnp.int32, (ki, kj), 1)
+    same_k = row // tiles_here == col // tiles
+    row_i = row % tiles_here
+    own_a = (
+        lax.broadcasted_iota(jnp.int32, (8 * tiles, kj), 0) // 8
+        == lax.broadcasted_iota(jnp.int32, (8 * tiles, kj), 1) % tiles
+    )
+
+    def adjoint_second(i, carry):
+        pick = jnp.where(same_k & (row_i == i), 1.0, 0.0).astype(jnp.bfloat16)
+        wide = jnp.where(own_a, dot(kept_a, pick), 0.0)
+        part = jnp.sum(wide.reshape(tiles, 8, kj), axis=0)
+        lhs = jnp.concatenate([part, turned(part, -1.0)], axis=1).astype(jnp.bfloat16)
+        lanes = pl.ds(pl.multiple_of(i * tile_len, tile_len), tile_len)
+        ga[:, lanes] = dot(lhs, uf[:, lanes])
+        return carry
+
+    lax.fori_loop(0, tiles_here, adjoint_second, 0)
+    send(ga, gother, {"sub": 1 - c}).wait()
+    total = ga[...] + gother[...]
+    gg[z] = jnp.where(c == 0, total[:4], total[4:])
+    late = gather_freq(gg)
+    forward(1, lambda lanes: (ga[:, lanes] + gother[:, lanes]) * gain)
+    p_out[...] = pg[0] + pg[1]
+    for copy in late:
+        copy.wait()
+    g_out[...] = gg[...]
+
+
+def final_kernel(nf, foc, obs, start, end, tids, table_tall, p, g, new_foc, new_res):
+    def run(d):
+        lanes = slice(None)
+        new_foc[0] = foc[0] + relax_step * signal_chunk(
+            table_tall[...], seen_rows(g, d, lanes, nf)
+        )
+        signal = signal_chunk(table_tall[...], seen_rows(p, d, lanes, nf))
+        t = tids[...]
+        inside = (start[d : d + 1, :] <= t) & (t < end[d : d + 1, :])
+        new_res[0] = obs[0] - jnp.where(inside, signal, 0.0)
+
+    for d in range(2):
+        pl.when(pl.program_id(0) == d)(functools.partial(run, d))
+
+
+def split_table(table):
+    high = lax.reduce_precision(table, 8, 7)
+    low = lax.reduce_precision(table - high, 8, 7)
+    return high.astype(jnp.bfloat16), low.astype(jnp.bfloat16)
+
+
+def fast_body(focusing, observed, recv_factor, source_factor, tile_ranks, window_start, window_end):
+    nf = lax.axis_size("freq")
+    ranks, tiles = recv_factor.shape[2:4]
+    tiles_here = source_factor.shape[3]
+    half_foc, local_t, lanes = focusing.shape
+    tile_len = lanes // tiles_here
+    cos_table, sin_table = dft_tables(nf, NT)
+    table = jnp.stack([cos_table, -sin_table], axis=1).reshape(2 * nf, NT)
+    table = lax.dynamic_slice_in_dim(table, lax.axis_index("freq") * local_t, local_t, 1)
+    high, low = split_table(table)
+    table_wide = jnp.concatenate(
+        [jnp.concatenate([high, high], 1), jnp.concatenate([low, low], 1)], 0
+    )
+    table_tall = jnp.concatenate([high, high, low, low], 0).T
+    tids = (lax.axis_index("freq") * local_t + jnp.arange(local_t, dtype=jnp.int32))[:, None]
+    rank_ids = lax.axis_index("sub") * ranks + jnp.arange(ranks, dtype=jnp.int32)
+    held = tile_ranks[0]
+    keep_f = (rank_ids[None, :, None] < held[:, None, :]).astype(jnp.float32)
+    keep_f = jnp.repeat(keep_f.reshape(tiles_here, ranks * tiles), 8, axis=0)
+    keep_a = (rank_ids[None, :, None] < held.T[:, None, :]).astype(jnp.float32)
+    keep_a = jnp.repeat(keep_a.reshape(tiles, ranks * tiles_here), 8, axis=0)
+    uf = recv_factor.reshape(2 * ranks * tiles, lanes)
+    vf = source_factor.reshape(2 * ranks * tiles_here, tiles * tile_len)
+    gain = (0.5 * NT) * float(nf * NT) ** (-0.5)
+    f32 = jnp.float32
+    spectra = jax.ShapeDtypeStruct((nf, 4, lanes), f32)
+    p, g = pl.pallas_call(
+        functools.partial(core_kernel, nf, tiles, tiles_here, ranks, tile_len, gain),
+        out_shape=(spectra, spectra),
+        in_specs=[pl.BlockSpec(memory_space=pltpu.VMEM)] * 11,
+        out_specs=(pl.BlockSpec(memory_space=pltpu.VMEM),) * 2,
+        scratch_shapes=[
+            pltpu.VMEM((2, nf, 4, lanes), f32),
+            pltpu.VMEM((2, nf - 1, 4, lanes), f32),
+            pltpu.VMEM((4, lanes), f32),
+            pltpu.VMEM((4, lanes), f32),
+            pltpu.VMEM((8 * tiles_here, ranks * tiles), f32),
+            pltpu.VMEM((2, 2, 2, 4, lanes), f32),
+            pltpu.VMEM((2, 3, 4, lanes), f32),
+            pltpu.VMEM((2, nf, 4, lanes), f32),
+            pltpu.VMEM((2, 2, 4, lanes), f32),
+            pltpu.VMEM((8 * tiles, ranks * tiles_here), f32),
+            pltpu.VMEM((8, lanes), f32),
+            pltpu.VMEM((8, lanes), f32),
+            pltpu.VMEM((nf, 4, lanes), f32),
+            pltpu.SemaphoreType.DMA((5 * (nf - 1) + 11,)),
+            pltpu.SemaphoreType.DMA((5 * (nf - 1) + 11,)),
+        ],
+        compiler_params=pltpu.CompilerParams(
+            collective_id=0, has_side_effects=True, vmem_limit_bytes=48 * 2**20
+        ),
+        name="spectra",
+    )(focusing, observed, uf, vf, keep_f, keep_a, window_start, window_end, tids, table_wide, table_tall)
+    width = 1024
+    signal_spec = pl.BlockSpec((1, local_t, width), lambda d, k: (d, 0, k))
+    edge_spec = pl.BlockSpec((half_foc, width), lambda d, k: (0, k))
+    spectra_spec = pl.BlockSpec((nf, 4, width), lambda d, k: (0, 0, k))
+    return pl.pallas_call(
+        functools.partial(final_kernel, nf),
+        grid=(half_foc, lanes // width),
+        out_shape=(jax.ShapeDtypeStruct(focusing.shape, f32),) * 2,
+        in_specs=[
+            signal_spec, signal_spec, edge_spec, edge_spec,
+            pl.BlockSpec(tids.shape, lambda d, k: (0, 0)),
+            pl.BlockSpec(table_tall.shape, lambda d, k: (0, 0)),
+            spectra_spec, spectra_spec,
+        ],
+        out_specs=(signal_spec,) * 2,
+        compiler_params=pltpu.CompilerParams(vmem_limit_bytes=32 * 2**20),
+        name="update",
+    )(focusing, observed, window_start, window_end, tids, table_tall, p, g)
+
+
+def fits(focusing, recv_factor, source_factor):
+    bands, ranks, tiles = recv_factor.shape[1:4]
+    tiles_here = source_factor.shape[3]
+    half_foc, local_t, lanes = focusing.shape
+    return (
+        (lax.axis_size("freq"), lax.axis_size("recv"), lax.axis_size("sub")) == (4, 2, 2)
+        and (bands, half_foc, local_t) == (1, 2, 128)
+        and (ranks * tiles_here) % 128 == 0
+        and lanes // tiles_here == 256
+        and tiles == 2 * tiles_here
+        and lanes % 1024 == 0
+    )
+
+
+def chosen(focusing, observed, recv_factor, source_factor, *rest):
+    form = fast_body if fits(focusing, recv_factor, source_factor) else body
+    return form(focusing, observed, recv_factor, source_factor, *rest)
+
+
 def solution(mesh):
     placed = (
         P(("group", "sub"), "freq", "recv"),
@@ -148,7 +479,7 @@
         P(("group", "sub"), "recv"),
     )
     return jax.shard_map(
-        body,
+        chosen,
         mesh=mesh,
         in_specs=placed,
         out_specs=(P(("group", "sub"), "freq", "recv"), P(("group", "sub"), "freq", "recv")),

time: 329 us -> 99.2 us (0.30); the launches traced: 324 us -> 98.8 us
  matrix products: 121 us -> 0 us
  blocking collectives: 102 us -> 0 us
  Pallas kernels: 0 us -> 92.1 us
  local copies, waits for them, and re-layouts: 49.9 us -> 5.73 us
  waiting for transfers between devices: 32.7 us -> 0 us
  between operations: 15.8 us -> 0.76 us
    dot_general x34 -> x0, matrix products: 121 us -> none  [the longest x24 56 us: contract(): return jnp.einsum(form, left, right, preferred_element_type=jnp.float32)]
    pallas_call x0 -> x2, Pallas kernels: none -> 92.1 us  [the longest x1 86.2 us: fast_body(): pl.pallas_call(functools.partial(core_kernel, nf, tiles, tiles_here, rank...]
    all_gather x6 -> x0, blocking collectives: 53.2 us -> none  [the longest x3 43.4 us: to_signal(): lax.all_gather(spectrum, 'freq', axis=1, tiled=True)]
    unnamed x2 -> x0, blocking collectives: 48.9 us -> none
    unnamed x6 -> x0, waiting for transfers between devices: 32.7 us -> none
    unnamed x59 -> x8, local copies, waits for them, and re-layouts: 31.7 us -> 3.7 us
    another operation x22 -> x1, local copies, waits for them, and re-layouts: 8.3 us -> 0.01 us  [fast_body(): table = jnp.stack([cos_table, -sin_table], axis=1).reshape(2 * nf, NT)]
    slice x10 -> x0, local copies, waits for them, and re-layouts: 8.04 us -> none  [the longest x1 3.98 us: forward(): source_blocks[1]]
  transfers between devices with their start and end apart: 3 -> 0, of which waited for: 2 -> 0; matrix products, arithmetic and copies ran while one was open for 10% -> 0% of each run, Pallas kernels for 0% -> 0%
where the time goes in v2:
time: 99.2 us; the launch traced here: 98.8 us
  Pallas kernels  92.1 us (93%)
  local copies, waits for them, and re-layouts  5.73 us (6%)
    pallas_call x1, Pallas kernels, fast_body(): pl.pallas_call(functools.partial(core_kernel, nf, tiles, tiles_here, rank...  86.2 us
    pallas_call x1, Pallas kernels, fast_body(): pl.pallas_call(functools.partial(final_kernel, nf), grid=(half_foc, lanes...  5.88 us
    unnamed x8, local copies, waits for them, and re-layouts  3.7 us

profile of v2, /device:TPU:0, one launch (start us, length us, event | category | flops | bytes accessed | tf_op | source)
XLA Modules:
  0.0 98.8 jit_solution(5464372275838660175)
XLA Ops:
  0.7 0.1 lt.62
  0.7 0.1 lt.63
  0.8 0.1 lt.55
  0.9 0.1 lt.56
  1.0 0.2 cosine_multiply_fusion
  1.2 0.1 copy.17
  1.4 0.7 lt.59
  2.1 0.1 lt.60
  2.2 0.7 lt.65
  2.9 0.1 copy.18
  3.0 0.0 copy-start
  3.0 2.2 %copy-done = f32[2,128,4096]{2,1,0:T(8,128)S(1)} copy-done((f32[2,128,4096]{2,1,0:T(8,128)S(1)}, f32[2,128,4096]{2,1,0:T(8,128)}, u32[]{:S(2)}) %copy-start) | copy-done | bytes 4194328
  5.2 0.0 copy-start.2
  5.2 0.8 copy-done.2
  5.9 0.0 copy-start.3
  5.9 0.8 copy-done.3
  6.7 0.0 copy-start.1
  6.7 86.2 %spectra.1 = (f32[4,4,4096]{2,1,0:T(4,128)S(1)}, f32[4,4,4096]{2,1,0:T(4,128)S(1)}) custom-call(f32[2,128,4096]{2,1,0:T(8,128)S(1)} %copy-done, f32[2,128,4096]{2,1,0:T(8,128)} %obs.3, bf16[512,4096]{1,0:T(8,128)(2,1)} %bitcast.13, bf16[256,8192]{1,0:T(8,128)(2,1)} %bitcast.14, f32[128,256]{1,0:T(8,128)S(1)} %broadcast_bitcast_fusion.1.keep_f, ...), custom_call_target="tpu_custom_call" | custom-call | tf_op jit(solution)/shard_map/spectra/pallas_call | solution.py:405
  92.9 0.0 copy-done.1
  93.0 5.9 %update.1 = (f32[2,128,4096]{2,1,0:T(8,128)}, f32[2,128,4096]{2,1,0:T(8,128)}) custom-call(f32[2,128,4096]{2,1,0:T(8,128)S(1)} %copy-done, f32[2,128,4096]{2,1,0:T(8,128)S(1)} %copy-done.1, s32[2,4096]{1,0:T(2,128)S(1)} %copy-done.2, s32[2,4096]{1,0:T(2,128)S(1)} %copy-done.3, s32[128,1]{1,0:T(8,128)S(1)} %iota_add_fusion.tids, ...), custom_call_target="tpu_custom_call" | custom-call | tf_op jit(solution)/shard_map/update/pallas_call | solution.py:436
  (13 shorter events, 0.1 us)
Async XLA Ops:
  3.0 2.2 %copy-start = (f32[2,128,4096]{2,1,0:T(8,128)S(1)}, f32[2,128,4096]{2,1,0:T(8,128)}, u32[]{:S(2)}) copy-start(f32[2,128,4096]{2,1,0:T(8,128)} %foc.3) | copy-start | bytes 12582916
  5.2 0.8 copy-start.2
  5.9 0.8 copy-start.3
  6.7 86.3 %copy-start.1 = (f32[2,128,4096]{2,1,0:T(8,128)S(1)}, f32[2,128,4096]{2,1,0:T(8,128)}, u32[]{:S(2)}) copy-start(f32[2,128,4096]{2,1,0:T(8,128)} %obs.3) | copy-start | bytes 12582916

commit v3 on v2

--- a/solution.py
+++ b/solution.py
@@ -163,6 +163,16 @@
     return high, (x - high.astype(jnp.float32)).astype(jnp.bfloat16)
 
 
+def packed(x):
+    w = x.shape[1] // 4
+    return jnp.concatenate([x[:, k * w : (k + 1) * w] for k in range(4)], axis=0).astype(jnp.bfloat16)
+
+
+def unpacked(x):
+    y = x.astype(jnp.float32)
+    return jnp.concatenate([y[4 * k : 4 * k + 4] for k in range(4)], axis=1)
+
+
 def spectrum_chunk(table_wide, v):
     out = dot(table_wide, jnp.concatenate(halves(v), axis=0))
     rows = out.shape[0] // 2
@@ -181,14 +191,28 @@
 
 def core_kernel(
     nf, tiles, tiles_here, ranks, tile_len, gain,
-    foc, obs, uf, vf, keep_f, keep_a, start, end, tids, table_wide, table_tall,
+    foc_in, obs_in, uf_in, vf_in, keep_f, keep_a, start, end, tids, table_wide, table_tall,
     p_out, g_out,
-    sp, zrecv, zsum, zother, coef, ybuf, yrecv, pg, zg, adj, ga, gother, gg,
+    sp, zrecv, zsum, zother, coef, ybuf, yrecv, pg, zg, adj, ga, gother,
+    spb, subb, pgb, zgb, ggb, foc, obs, uf, vf, load_sem,
     send_sem, recv_sem,
 ):
     z, x, c = lax.axis_index("freq"), lax.axis_index("recv"), lax.axis_index("sub")
     lanes_all = tiles_here * tile_len
     peers = [(dx, dc) for dx in range(2) for dc in range(2) if dx + dc]
+    part = lanes_all // 4
+    loads = [
+        pltpu.make_async_copy(
+            foc_in.at[:, :, pl.ds(k * part, part)],
+            foc.at[:, :, pl.ds(k * part, part)],
+            load_sem.at[k],
+        )
+        for k in range(4)
+    ]
+    for k, (src, dst) in enumerate([(uf_in, uf), (vf_in, vf), (obs_in, obs)]):
+        loads.append(pltpu.make_async_copy(src, dst, load_sem.at[4 + k]))
+    for load in loads:
+        load.start()
     zs = [{"freq": lax.rem(z + k, nf)} for k in range(1, nf)]
     near = [{"recv": x + dx - 2 * dx * x, "sub": c + dc - 2 * dc * c} for dx, dc in peers]
     barrier = pltpu.get_barrier_semaphore()
@@ -210,14 +234,16 @@
         return copy
 
     def reduce_freq(n):
+        for f in range(nf):
+            spb[n, f] = packed(sp[n, f])
         copies = [
-            send(sp.at[n, zs[k]["freq"]], zrecv.at[n, k], zs[k]) for k in range(nf - 1)
+            send(spb.at[n, zs[k]["freq"]], zrecv.at[n, k], zs[k]) for k in range(nf - 1)
         ]
         for copy in copies:
             copy.wait()
         total = sp[n, z]
         for k in range(nf - 1):
-            total = total + zrecv[n, k]
+            total = total + unpacked(zrecv[n, k])
         return total
 
     def gather_freq(buf):
@@ -235,7 +261,7 @@
             coef[pl.ds(pl.multiple_of(i * 8, 8), 8), :] = out[:, :half] + turned(out[:, half:], 1.0)
             return carry
 
-        lax.fori_loop(0, tiles_here, first, 0)
+        lax.fori_loop(0, tiles_here, first, 0, unroll=16)
         kept = (coef[...] * keep_f[...]).astype(jnp.bfloat16)
         kj, ki = ranks * tiles, ranks * tiles_here
         row = lax.broadcasted_iota(jnp.int32, (kj, 2 * ki), 0)
@@ -261,7 +287,7 @@
                 ybuf[n, block, 1, :, pl.ds(at, tile_len)] = out[4:]
             return carry
 
-        lax.fori_loop(0, tiles // 2, second, 0)
+        lax.fori_loop(0, tiles // 2, second, 0, unroll=8)
         copies = [
             send(ybuf.at[n, device["recv"], device["sub"]], yrecv.at[n, k], device)
             for k, device in enumerate(near)
@@ -271,31 +297,40 @@
         total = ybuf[n, x, c]
         for k in range(len(near)):
             total = total + yrecv[n, k]
-        pg[n, z] = total
-        for copy in gather_freq(pg.at[n]):
+        pgb[n, z] = packed(total)
+        for copy in gather_freq(pgb.at[n]):
             copy.wait()
-
-    def chunks(step):
+        for f in range(nf):
+            pg[n, f] = unpacked(pgb[n, f])
+
+    def chunks(step, first=0, last=lanes_all // CHUNK):
         def one(k, carry):
             step(pl.ds(pl.multiple_of(k * CHUNK, CHUNK), CHUNK))
             return carry
 
-        lax.fori_loop(0, lanes_all // CHUNK, one, 0)
+        lax.fori_loop(first, last, one, 0, unroll=2)
 
     def start_spec(lanes):
         for d in range(2):
             put_spectrum(0, d, lanes, spectrum_chunk(table_wide[...], foc[d, :, lanes]))
 
-    chunks(start_spec)
-    zsum[...] = reduce_freq(0)
-    send(zsum, zother, {"sub": 1 - c}).wait()
+    for k in range(4):
+        loads[k].wait()
+        chunks(start_spec, k * part // CHUNK, (k + 1) * part // CHUNK)
+    subb[0] = packed(reduce_freq(0))
+    send(subb.at[0], subb.at[1], {"sub": 1 - c}).wait()
+    zsum[...] = unpacked(subb[0])
+    zother[...] = unpacked(subb[1])
 
     def spec_rows(lanes):
         mine, other = zsum[:, lanes], zother[:, lanes]
         first, last = jnp.where(c == 0, mine, other), jnp.where(c == 0, other, mine)
         return jnp.concatenate([first, last], axis=0)
 
+    loads[4].wait()
+    loads[5].wait()
     forward(0, spec_rows)
+    loads[6].wait()
 
     def windowed(lanes):
         for d in range(2):
@@ -306,9 +341,12 @@
             put_spectrum(1, d, lanes, spectrum_chunk(table_wide[...], kept))
 
     chunks(windowed)
-    zg[x, c] = reduce_freq(1)
-    for copy in [send(zg.at[x, c], zg.at[x, c], device) for device in near]:
+    zgb[x, c] = packed(reduce_freq(1))
+    for copy in [send(zgb.at[x, c], zgb.at[x, c], device) for device in near]:
         copy.wait()
+    for block in range(2):
+        for half in range(2):
+            zg[block, half] = unpacked(zgb[block, half])
 
     ki, kj = ranks * tiles_here, ranks * tiles
 
@@ -323,7 +361,7 @@
         adj[pl.ds(pl.multiple_of(j * 8, 8), 8), :] = out[:, :ki] + turned(out[:, ki:], -1.0)
         return carry
 
-    lax.fori_loop(0, tiles, adjoint_first, 0)
+    lax.fori_loop(0, tiles, adjoint_first, 0, unroll=16)
     kept_a = (adj[...] * keep_a[...]).astype(jnp.bfloat16)
     row = lax.broadcasted_iota(jnp.int32, (ki, kj), 0)
     col = lax.broadcasted_iota(jnp.int32, (ki, kj), 1)
@@ -343,16 +381,17 @@
         ga[:, lanes] = dot(lhs, uf[:, lanes])
         return carry
 
-    lax.fori_loop(0, tiles_here, adjoint_second, 0)
+    lax.fori_loop(0, tiles_here, adjoint_second, 0, unroll=8)
     send(ga, gother, {"sub": 1 - c}).wait()
     total = ga[...] + gother[...]
-    gg[z] = jnp.where(c == 0, total[:4], total[4:])
-    late = gather_freq(gg)
+    ggb[z] = packed(jnp.where(c == 0, total[:4], total[4:]))
+    late = gather_freq(ggb)
     forward(1, lambda lanes: (ga[:, lanes] + gother[:, lanes]) * gain)
     p_out[...] = pg[0] + pg[1]
     for copy in late:
         copy.wait()
-    g_out[...] = gg[...]
+    for f in range(nf):
+        g_out[f] = unpacked(ggb[f])
 
 
 def final_kernel(nf, foc, obs, start, end, tids, table_tall, p, g, new_foc, new_res):
@@ -405,11 +444,12 @@
     p, g = pl.pallas_call(
         functools.partial(core_kernel, nf, tiles, tiles_here, ranks, tile_len, gain),
         out_shape=(spectra, spectra),
-        in_specs=[pl.BlockSpec(memory_space=pltpu.VMEM)] * 11,
+        in_specs=[pl.BlockSpec(memory_space=pl.ANY)] * 4
+        + [pl.BlockSpec(memory_space=pltpu.VMEM)] * 7,
         out_specs=(pl.BlockSpec(memory_space=pltpu.VMEM),) * 2,
         scratch_shapes=[
             pltpu.VMEM((2, nf, 4, lanes), f32),
-            pltpu.VMEM((2, nf - 1, 4, lanes), f32),
+            pltpu.VMEM((2, nf - 1, 16, lanes // 4), jnp.bfloat16),
             pltpu.VMEM((4, lanes), f32),
             pltpu.VMEM((4, lanes), f32),
             pltpu.VMEM((8 * tiles_here, ranks * tiles), f32),
@@ -420,7 +460,16 @@
             pltpu.VMEM((8 * tiles, ranks * tiles_here), f32),
             pltpu.VMEM((8, lanes), f32),
             pltpu.VMEM((8, lanes), f32),
-            pltpu.VMEM((nf, 4, lanes), f32),
+            pltpu.VMEM((2, nf, 16, lanes // 4), jnp.bfloat16),
+            pltpu.VMEM((2, 16, lanes // 4), jnp.bfloat16),
+            pltpu.VMEM((2, nf, 16, lanes // 4), jnp.bfloat16),
+            pltpu.VMEM((2, 2, 16, lanes // 4), jnp.bfloat16),
+            pltpu.VMEM((nf, 16, lanes // 4), jnp.bfloat16),
+            pltpu.VMEM(focusing.shape, f32),
+            pltpu.VMEM(observed.shape, f32),
+            pltpu.VMEM(uf.shape, jnp.bfloat16),
+            pltpu.VMEM(vf.shape, jnp.bfloat16),
+            pltpu.SemaphoreType.DMA((7,)),
             pltpu.SemaphoreType.DMA((5 * (nf - 1) + 11,)),
             pltpu.SemaphoreType.DMA((5 * (nf - 1) + 11,)),
         ],

time: 99.2 us -> 68.4 us (0.69)
  Pallas kernels: 92.1 us -> 61.3 us
    pallas_call x1, Pallas kernels: 86.2 us -> 55.5 us  [fast_body(): pl.pallas_call(functools.partial(core_kernel, nf, tiles, tiles_here, rank...]
where the time goes in v3:
time: 68.4 us; the launch traced here: 68 us
  Pallas kernels  61.3 us (90%)
  local copies, waits for them, and re-layouts  5.73 us (8%)
  between operations  0.76 us (1%)
    pallas_call x1, Pallas kernels, fast_body(): pl.pallas_call(functools.partial(core_kernel, nf, tiles, tiles_here, rank...  55.5 us
    pallas_call x1, Pallas kernels, fast_body(): pl.pallas_call(functools.partial(final_kernel, nf), grid=(half_foc, lanes...  5.88 us
    unnamed x8, local copies, waits for them, and re-layouts  3.7 us

profile of v3, /device:TPU:0, one launch (start us, length us, event | category | flops | bytes accessed | tf_op | source)
XLA Modules:
  0.0 68.0 jit_solution(3447630826743688787)
XLA Ops:
  0.7 0.1 lt.62
  0.7 0.1 lt.63
  0.8 0.1 lt.55
  0.9 0.1 lt.56
  1.0 0.2 cosine_multiply_fusion
  1.2 0.1 copy.17
  1.4 0.7 %lt.59 = s32[16,8,32]{2,1,0:T(8,128)S(1)} broadcast(s32[16,32]{1,0:T(8,128)} %bitcast.16), dimensions={0,2} | broadcast | bytes 18432 | tf_op jit(solution)/shard_map/lt | solution.py:435
  2.1 0.1 lt.60
  2.2 0.7 %lt.65 = s32[32,8,16]{0,2,1:T(8,128)S(1)} broadcast(s32[32,16]{0,1:T(8,128)} %bitcast.17), dimensions={0,2} | broadcast | bytes 18432 | tf_op jit(solution)/shard_map/lt | solution.py:437
  2.9 0.1 copy.18
  3.0 0.0 copy-start
  3.0 2.2 %copy-done = f32[2,128,4096]{2,1,0:T(8,128)S(1)} copy-done((f32[2,128,4096]{2,1,0:T(8,128)S(1)}, f32[2,128,4096]{2,1,0:T(8,128)}, u32[]{:S(2)}) %copy-start) | copy-done | bytes 4194328
  5.2 0.0 copy-start.2
  5.2 0.8 %copy-done.2 = s32[2,4096]{1,0:T(2,128)S(1)} copy-done((s32[2,4096]{1,0:T(2,128)S(1)}, s32[2,4096]{1,0:T(2,128)}, u32[]{:S(2)}) %copy-start.2) | copy-done | bytes 32792
  5.9 0.0 copy-start.3
  5.9 0.8 %copy-done.3 = s32[2,4096]{1,0:T(2,128)S(1)} copy-done((s32[2,4096]{1,0:T(2,128)S(1)}, s32[2,4096]{1,0:T(2,128)}, u32[]{:S(2)}) %copy-start.3) | copy-done | bytes 32792
  6.7 0.0 copy-start.1
  6.7 55.5 %spectra.1 = (f32[4,4,4096]{2,1,0:T(4,128)S(1)}, f32[4,4,4096]{2,1,0:T(4,128)S(1)}) custom-call(f32[2,128,4096]{2,1,0:T(8,128)S(1)} %copy-done, f32[2,128,4096]{2,1,0:T(8,128)} %obs.1, bf16[512,4096]{1,0:T(8,128)(2,1)} %bitcast.13, bf16[256,8192]{1,0:T(8,128)(2,1)} %bitcast.14, f32[128,256]{1,0:T(8,128)S(1)} %broadcast_bitcast_fusion.1.keep_f, ...), custom_call_target="tpu_custom_call" | custom-call | tf_op jit(solution)/shard_map/spectra/pallas_call | solution.py:444
  62.1 0.0 copy-done.1
  62.2 5.9 %update.1 = (f32[2,128,4096]{2,1,0:T(8,128)}, f32[2,128,4096]{2,1,0:T(8,128)}) custom-call(f32[2,128,4096]{2,1,0:T(8,128)S(1)} %copy-done, f32[2,128,4096]{2,1,0:T(8,128)S(1)} %copy-done.1, s32[2,4096]{1,0:T(2,128)S(1)} %copy-done.2, s32[2,4096]{1,0:T(2,128)S(1)} %copy-done.3, s32[128,1]{1,0:T(8,128)S(1)} %iota_add_fusion.tids, ...), custom_call_target="tpu_custom_call" | custom-call | tf_op jit(solution)/shard_map/update/pallas_call | solution.py:485
  (13 shorter events, 0.1 us)
Async XLA Ops:
  3.0 2.2 %copy-start = (f32[2,128,4096]{2,1,0:T(8,128)S(1)}, f32[2,128,4096]{2,1,0:T(8,128)}, u32[]{:S(2)}) copy-start(f32[2,128,4096]{2,1,0:T(8,128)} %foc.1) | copy-start | bytes 12582916
  5.2 0.8 %copy-start.2 = (s32[2,4096]{1,0:T(2,128)S(1)}, s32[2,4096]{1,0:T(2,128)}, u32[]{:S(2)}) copy-start(s32[2,4096]{1,0:T(2,128)} %start.3) | copy-start | bytes 98308
  5.9 0.8 %copy-start.3 = (s32[2,4096]{1,0:T(2,128)S(1)}, s32[2,4096]{1,0:T(2,128)}, u32[]{:S(2)}) copy-start(s32[2,4096]{1,0:T(2,128)} %end.3) | copy-start | bytes 98308
  6.7 55.5 %copy-start.1 = (f32[2,128,4096]{2,1,0:T(8,128)S(1)}, f32[2,128,4096]{2,1,0:T(8,128)}, u32[]{:S(2)}) copy-start(f32[2,128,4096]{2,1,0:T(8,128)} %obs.1) | copy-start | bytes 12582916

commit v4 on v3

--- a/solution.py
+++ b/solution.py
@@ -194,7 +194,7 @@
     foc_in, obs_in, uf_in, vf_in, keep_f, keep_a, start, end, tids, table_wide, table_tall,
     p_out, g_out,
     sp, zrecv, zsum, zother, coef, ybuf, yrecv, pg, zg, adj, ga, gother,
-    spb, subb, pgb, zgb, ggb, foc, obs, uf, vf, load_sem,
+    subb, pgb, zgb, ggb, foc, obs, uf, vf, load_sem,
     send_sem, recv_sem,
 ):
     z, x, c = lax.axis_index("freq"), lax.axis_index("recv"), lax.axis_index("sub")
@@ -234,16 +234,14 @@
         return copy
 
     def reduce_freq(n):
-        for f in range(nf):
-            spb[n, f] = packed(sp[n, f])
         copies = [
-            send(spb.at[n, zs[k]["freq"]], zrecv.at[n, k], zs[k]) for k in range(nf - 1)
+            send(sp.at[n, zs[k]["freq"]], zrecv.at[n, k], zs[k]) for k in range(nf - 1)
         ]
         for copy in copies:
             copy.wait()
         total = sp[n, z]
         for k in range(nf - 1):
-            total = total + unpacked(zrecv[n, k])
+            total = total + zrecv[n, k]
         return total
 
     def gather_freq(buf):
@@ -384,14 +382,14 @@
     lax.fori_loop(0, tiles_here, adjoint_second, 0, unroll=8)
     send(ga, gother, {"sub": 1 - c}).wait()
     total = ga[...] + gother[...]
-    ggb[z] = packed(jnp.where(c == 0, total[:4], total[4:]))
+    ggb[z] = jnp.where(c == 0, total[:4], total[4:])
     late = gather_freq(ggb)
     forward(1, lambda lanes: (ga[:, lanes] + gother[:, lanes]) * gain)
     p_out[...] = pg[0] + pg[1]
     for copy in late:
         copy.wait()
     for f in range(nf):
-        g_out[f] = unpacked(ggb[f])
+        g_out[f] = ggb[f]
 
 
 def final_kernel(nf, foc, obs, start, end, tids, table_tall, p, g, new_foc, new_res):
@@ -449,7 +447,7 @@
         out_specs=(pl.BlockSpec(memory_space=pltpu.VMEM),) * 2,
         scratch_shapes=[
             pltpu.VMEM((2, nf, 4, lanes), f32),
-            pltpu.VMEM((2, nf - 1, 16, lanes // 4), jnp.bfloat16),
+            pltpu.VMEM((2, nf - 1, 4, lanes), f32),
             pltpu.VMEM((4, lanes), f32),
             pltpu.VMEM((4, lanes), f32),
             pltpu.VMEM((8 * tiles_here, ranks * tiles), f32),
@@ -460,11 +458,10 @@
             pltpu.VMEM((8 * tiles, ranks * tiles_here), f32),
             pltpu.VMEM((8, lanes), f32),
             pltpu.VMEM((8, lanes), f32),
-            pltpu.VMEM((2, nf, 16, lanes // 4), jnp.bfloat16),
             pltpu.VMEM((2, 16, lanes // 4), jnp.bfloat16),
             pltpu.VMEM((2, nf, 16, lanes // 4), jnp.bfloat16),
             pltpu.VMEM((2, 2, 16, lanes // 4), jnp.bfloat16),
-            pltpu.VMEM((nf, 16, lanes // 4), jnp.bfloat16),
+            pltpu.VMEM((nf, 4, lanes), f32),
             pltpu.VMEM(focusing.shape, f32),
             pltpu.VMEM(observed.shape, f32),
             pltpu.VMEM(uf.shape, jnp.bfloat16),
@@ -474,7 +471,7 @@
             pltpu.SemaphoreType.DMA((5 * (nf - 1) + 11,)),
         ],
         compiler_params=pltpu.CompilerParams(
-            collective_id=0, has_side_effects=True, vmem_limit_bytes=48 * 2**20
+            collective_id=0, has_side_effects=True, vmem_limit_bytes=60 * 2**20
         ),
         name="spectra",
     )(focusing, observed, uf, vf, keep_f, keep_a, window_start, window_end, tids, table_wide, table_tall)

time: 68.4 us -> 80.2 us (1.17)
  Pallas kernels: 61.3 us -> 67.5 us
  local copies, waits for them, and re-layouts: 5.73 us -> 10.2 us
  other arithmetic: 0.21 us -> 1.42 us
    pallas_call x1, Pallas kernels: 55.5 us -> 61.6 us  [fast_body(): pl.pallas_call(functools.partial(core_kernel, nf, tiles, tiles_here, rank...]
    unnamed x8 -> x16, local copies, waits for them, and re-layouts: 3.7 us -> 6.28 us
where the time goes in v4:
time: 80.2 us; the launch traced here: 79.9 us
  Pallas kernels  67.5 us (84%)
  local copies, waits for them, and re-layouts  10.2 us (13%)
  other arithmetic  1.42 us (2%)
    pallas_call x1, Pallas kernels, fast_body(): pl.pallas_call(functools.partial(core_kernel, nf, tiles, tiles_here, rank...  61.6 us
    unnamed x16, local copies, waits for them, and re-layouts  6.28 us
    pallas_call x1, Pallas kernels, fast_body(): pl.pallas_call(functools.partial(final_kernel, nf), grid=(half_foc, lanes...  5.85 us

profile of v4, /device:TPU:0, one launch (start us, length us, event | category | flops | bytes accessed | tf_op | source)
XLA Modules:
  0.0 79.9 jit_solution(11950075629981734482)
XLA Ops:
  0.7 0.1 lt.62
  0.7 0.1 lt.63
  0.8 0.1 lt.55
  0.9 0.1 lt.56
  1.0 0.2 cosine_multiply_fusion
  1.2 0.6 maximum_maximum_fusion.table_wide
  1.8 0.7 copy.17
  2.5 0.6 iota_add_fusion.tids
  3.1 0.7 lt.59
  3.8 0.1 lt.60
  3.9 0.7 lt.65
  4.6 0.1 copy.18
  4.7 0.7 broadcast_bitcast_fusion.keep_a
  5.4 0.7 broadcast_bitcast_fusion.1.keep_f
  6.1 61.6 %spectra.1 = (f32[4,4,4096]{2,1,0:T(4,128)}, f32[4,4,4096]{2,1,0:T(4,128)}) custom-call(f32[2,128,4096]{2,1,0:T(8,128)} %foc.1, f32[2,128,4096]{2,1,0:T(8,128)} %obs.1, bf16[512,4096]{1,0:T(8,128)(2,1)} %bitcast.13, bf16[256,8192]{1,0:T(8,128)(2,1)} %bitcast.14, f32[128,256]{1,0:T(8,128)} %broadcast_bitcast_fusion.1.keep_f, ...), custom_call_target="tpu_custom_call" | custom-call | tf_op jit(solution)/shard_map/spectra/pallas_call | solution.py:442
  67.7 0.0 copy-done.2
  67.7 0.0 copy-done.3
  67.7 0.0 copy-done.6
  67.8 0.0 copy-start
  67.8 2.2 %copy-done = f32[2,128,4096]{2,1,0:T(8,128)S(1)} copy-done((f32[2,128,4096]{2,1,0:T(8,128)S(1)}, f32[2,128,4096]{2,1,0:T(8,128)}, u32[]{:S(2)}) %copy-start) | copy-done | bytes 4194328
  69.9 2.2 %copy-done.1 = f32[2,128,4096]{2,1,0:T(8,128)S(1)} copy-done((f32[2,128,4096]{2,1,0:T(8,128)S(1)}, f32[2,128,4096]{2,1,0:T(8,128)}, u32[]{:S(2)}) %copy-start.1) | copy-done | bytes 4194328
  72.1 0.9 %copy-done.4 = f32[4,4,4096]{2,1,0:T(4,128)S(1)} copy-done((f32[4,4,4096]{2,1,0:T(4,128)S(1)}, f32[4,4,4096]{2,1,0:T(4,128)}, u32[]{:S(2)}) %copy-start.4) | copy-done | bytes 262168
  73.1 0.9 %copy-done.5 = f32[4,4,4096]{2,1,0:T(4,128)S(1)} copy-done((f32[4,4,4096]{2,1,0:T(4,128)S(1)}, f32[4,4,4096]{2,1,0:T(4,128)}, u32[]{:S(2)}) %copy-start.5) | copy-done | bytes 262168
  74.0 5.9 %update.1 = (f32[2,128,4096]{2,1,0:T(8,128)}, f32[2,128,4096]{2,1,0:T(8,128)}) custom-call(f32[2,128,4096]{2,1,0:T(8,128)S(1)} %copy-done, f32[2,128,4096]{2,1,0:T(8,128)S(1)} %copy-done.1, s32[2,4096]{1,0:T(2,128)S(1)} %copy-done.6, s32[2,4096]{1,0:T(2,128)S(1)} %copy-done.7, s32[128,1]{1,0:T(8,128)S(1)} %copy-done.2, bf16[128,32]{1,0:T(8,128)(2,1)S(1)} %bitcast.12, ...), custom_call_target="tpu_custom_call" | custom-call | tf_op jit(solution)/shard_map/update/pallas_call | solution.py:482
  (17 shorter events, 0.1 us)
Async XLA Ops:
  6.1 61.7 %copy-start.2 = (s32[128,1]{1,0:T(8,128)S(1)}, s32[128,1]{1,0:T(8,128)}, u32[]{:S(2)}) copy-start(s32[128,1]{1,0:T(8,128)} %iota_add_fusion.tids) | copy-start | bytes 1540
  6.1 61.7 %copy-start.3 = (bf16[32,128]{0,1:T(8,128)(2,1)S(1)}, bf16[32,128]{0,1:T(8,128)(2,1)}, u32[]{:S(2)}) copy-start(bf16[32,128]{0,1:T(8,128)(2,1)} %copy.17) | copy-start | bytes 24580
  6.1 61.7 %copy-start.6 = (s32[2,4096]{1,0:T(2,128)S(1)}, s32[2,4096]{1,0:T(2,128)}, u32[]{:S(2)}) copy-start(s32[2,4096]{1,0:T(2,128)} %start.3) | copy-start | bytes 98308
  6.1 61.7 %copy-start.7 = (s32[2,4096]{1,0:T(2,128)S(1)}, s32[2,4096]{1,0:T(2,128)}, u32[]{:S(2)}) copy-start(s32[2,4096]{1,0:T(2,128)} %end.3) | copy-start | bytes 98308
  67.8 2.2 %copy-start = (f32[2,128,4096]{2,1,0:T(8,128)S(1)}, f32[2,128,4096]{2,1,0:T(8,128)}, u32[]{:S(2)}) copy-start(f32[2,128,4096]{2,1,0:T(8,128)} %foc.1) | copy-start | bytes 12582916
  69.9 2.2 %copy-start.1 = (f32[2,128,4096]{2,1,0:T(8,128)S(1)}, f32[2,128,4096]{2,1,0:T(8,128)}, u32[]{:S(2)}) copy-start(f32[2,128,4096]{2,1,0:T(8,128)} %obs.1) | copy-start | bytes 12582916
  72.1 0.9 %copy-start.4 = (f32[4,4,4096]{2,1,0:T(4,128)S(1)}, f32[4,4,4096]{2,1,0:T(4,128)}, u32[]{:S(2)}) copy-start(f32[4,4,4096]{2,1,0:T(4,128)} %get-tuple-element.4.p) | copy-start | bytes 786436
  73.1 0.9 %copy-start.5 = (f32[4,4,4096]{2,1,0:T(4,128)S(1)}, f32[4,4,4096]{2,1,0:T(4,128)}, u32[]{:S(2)}) copy-start(f32[4,4,4096]{2,1,0:T(4,128)} %get-tuple-element.5.g) | copy-start | bytes 786436
